TPU v7x, 32 devices: a whole 2x2x4 slice. The times are simulated.
32 devices in a mesh: dp: 8 (over z, y), mp: 4 (over x, core).
Axes of the slice: x: 2, y: 2, z: 4, core: 2. Of those that a mesh axis runs over, the one named last changes fastest.
Arguments:
- tokens: bfloat16 [4096, 1152], P(('dp', 'mp')), may hold values from -6 to 6
- segment_ids: int32 [4096], P('dp'), may hold values from 0 to 2, as said below
- positions: int32 [4096], P('dp'), may hold values from 0 to 5118, as said below
- q_weight: bfloat16 [1152, 1024], P('dp', 'mp'), may hold values from -0.1875 to 0.1875
- kv_weight: bfloat16 [1152, 512], P('dp'), may hold values from -0.1875 to 0.1875
- o_weight: bfloat16 [1024, 1152], P('mp', 'dp'), may hold values from -0.1875 to 0.1875
- gate_up_weight: bfloat16 [2, 1152, 6912], P(None, 'dp', 'mp'), may hold values from -0.1875 to 0.1875
- down_weight: bfloat16 [6912, 1152], P('mp', 'dp'), may hold values from -0.078125 to 0.078125
- attn_pre_gain: bfloat16 [1152], P('dp'), may hold values from 0.25 to 1.75
- attn_post_gain: bfloat16 [1152], P('dp'), may hold values from 0.25 to 1.75
- ff_pre_gain: bfloat16 [1152], P('dp'), may hold values from 0.25 to 1.75
- ff_post_gain: bfloat16 [1152], P('dp'), may hold values from 0.25 to 1.75
- query_gain: bfloat16 [256], P('dp'), may hold values from 0.25 to 1.75
- key_gain: bfloat16 [256], P('dp'), may hold values from 0.25 to 1.75
- out_grad: bfloat16 [4096, 1152], P(('dp', 'mp')), may hold values from -6 to 6
Outputs:
- out: bfloat16 [4096, 1152], P(('dp', 'mp'))
- tokens_grad: float32 [4096, 1152], P(('dp', 'mp'))
- q_weight_grad: float32 [1152, 1024], P('dp', 'mp')
- kv_weight_grad: float32 [1152, 512], P('dp')
- o_weight_grad: float32 [1024, 1152], P('mp', 'dp')
- gate_up_weight_grad: float32 [2, 1152, 6912], P(None, 'dp', 'mp')
- down_weight_grad: float32 [6912, 1152], P('mp', 'dp')
- attn_pre_gain_grad: float32 [1152], P('dp')
- attn_post_gain_grad: float32 [1152], P('dp')
- ff_pre_gain_grad: float32 [1152], P('dp')
- ff_post_gain_grad: float32 [1152], P('dp')
- query_gain_grad: float32 [256], P('dp')
- key_gain_grad: float32 [256], P('dp')
Inputs may be any that keep to these rules, and one draw needn't show every extreme that they name: `segment_ids`: segment ids never fall; document 0 and document 2 each hold 1 to 256 tokens, document 1 the rest. Within a document, positions rise by one from token to token; document 0 starts at position 0, document 2 at 0 to 1023, and the last token of document 1 has position 5118.
All inputs are finite; a program needn't handle non-finite values.
Results may differ from a plain program's by a relative error of at most 0.028.
Values may be sent and summed in bfloat16 or wider, within the bound.
A program may use at most 128 MiB of HBM per device.

v0:
```python
from functools import partial
import jax
import jax.numpy as jnp
from jax import lax
from jax.sharding import PartitionSpec as P

WINDOW = 512
EPS = 1e-06
NEG = -1e30


def from_behind(value, axis, steps):
    count = lax.axis_size(axis)
    leading, last = (max(0, -steps), min(count, count - steps))
    return lax.ppermute(value, axis, [(source, source + steps) for source in range(leading, last)])


def shifted(value, axis, shift):
    count = lax.axis_size(axis)
    return lax.ppermute(value, axis, [(i, (i + shift) % count) for i in range(count)])


def gather_relative(value):
    count = lax.axis_size("mp")
    return [value] + [shifted(value, "mp", -step) for step in range(1, count)]


def gather_ordered(value):
    count = lax.axis_size("mp")
    rows = value.shape[0]
    me = lax.axis_index("mp")
    whole = jnp.zeros((count * rows,) + value.shape[1:], value.dtype)
    for step, block in enumerate(gather_relative(value)):
        owner = lax.rem(me + step, count)
        whole = lax.dynamic_update_slice_in_dim(whole, block, owner * rows, axis=0)
    return whole


def scatter_relative(blocks):
    total = blocks[0].astype(jnp.float32)
    for step in range(1, len(blocks)):
        total = total + shifted(blocks[step], "mp", step).astype(jnp.float32)
    return total


def scatter_ordered(value):
    count = lax.axis_size("mp")
    rows = value.shape[0] // count
    me = lax.axis_index("mp")
    return scatter_relative(
        [
            lax.dynamic_slice_in_dim(value, lax.rem(me + step, count) * rows, rows, axis=0)
            for step in range(count)
        ]
    )


def split_rows(value):
    rows = value.shape[0] // lax.axis_size("mp")
    return [value[i * rows : (i + 1) * rows] for i in range(lax.axis_size("mp"))]


def sum_over_mp(value):
    total = value.astype(jnp.float32)
    for step in range(1, lax.axis_size("mp")):
        total = total + shifted(value, "mp", step).astype(jnp.float32)
    return total


def normalize(value, gain):
    return value * lax.rsqrt(jnp.mean(value * value, axis=-1, keepdims=True) + EPS) * gain


def rotary_tables(positions, width):
    half_width = width // 2
    frequency = jnp.power(10000.0, -jnp.arange(half_width, dtype=jnp.float32) * (2.0 / width))
    angles = positions.astype(jnp.float32)[:, None] * frequency[None, :]
    return (jnp.cos(angles), jnp.sin(angles))


def rotate(value, cosine, sine):
    half_width = value.shape[-1] // 2
    first_half = value[..., :half_width]
    second_half = value[..., half_width:]
    return jnp.concatenate(
        [first_half * cosine - second_half * sine, second_half * cosine + first_half * sine],
        axis=-1,
    )


def prepare_head(pre_value, gain, cosine, sine):
    return rotate(normalize(pre_value, gain), cosine, sine)


def gated_units(gate, up_part):
    return jax.nn.gelu(gate, approximate=True) * up_part


def norm_back(value, gain, grad):
    unused, pull = jax.vjp(normalize, value, gain)
    return pull(grad)


def local(
    tokens,
    segment_ids,
    positions,
    q_weight,
    kv_weight,
    o_weight,
    gate_up_weight,
    down_weight,
    attn_pre_gain,
    attn_post_gain,
    ff_pre_gain,
    ff_post_gain,
    query_gain,
    key_gain,
    out_grad,
):
    rows = q_weight.shape[0]
    head_size = q_weight.shape[1]
    width = rows * lax.axis_size("dp")
    gain_rows = query_gain.shape[0]
    small_gains = [jnp.pad(item, (0, rows - gain_rows)) for item in (query_gain, key_gain)]
    gain_columns = jnp.stack(
        [attn_pre_gain, attn_post_gain, ff_pre_gain, ff_post_gain] + small_gains, axis=1
    )
    gain_columns = jnp.pad(gain_columns, ((0, 0), (0, 128 - gain_columns.shape[1])))
    packed = jnp.concatenate([q_weight, kv_weight, jnp.transpose(o_weight), gain_columns], axis=1)
    packed_full = lax.all_gather(packed, "dp", axis=0, tiled=True)
    gate_up_full = lax.all_gather(gate_up_weight, "dp", axis=1, tiled=True)
    down_full = lax.all_gather(down_weight, "dp", axis=1, tiled=True)
    joint_weight = packed_full[:, : 3 * head_size]
    output_turned = packed_full[:, 3 * head_size : 4 * head_size]
    gain_block = jnp.transpose(packed_full[:, 4 * head_size :]).astype(jnp.float32)
    gains = [gain_block[i] for i in range(4)] + [
        gain_block[i].reshape(-1, rows)[:, :gain_rows].reshape(-1) for i in (4, 5)
    ]
    length = segment_ids.shape[0]
    reach = -(-WINDOW // length)
    block_size = min(512, length)
    score_scale = head_size ** (-0.5)
    span = block_size + WINDOW
    cosine, sine = rotary_tables(positions, head_size)
    distance = (
        jnp.arange(block_size, dtype=jnp.int32)[:, None]
        + WINDOW
        - jnp.arange(span, dtype=jnp.int32)[None, :]
    )
    inside = (distance >= 0) & (distance < WINDOW)
    residual = tokens.astype(jnp.float32)
    attn_local = normalize(residual, gains[0]).astype(jnp.bfloat16)
    attn_in = gather_ordered(attn_local)
    projected = jnp.dot(attn_in, joint_weight, preferred_element_type=jnp.float32)
    query_pre = projected[:, :head_size]
    key_pre = projected[:, head_size : 2 * head_size]
    value_pre = projected[:, 2 * head_size :]
    queries = prepare_head(query_pre, gains[4], cosine, sine).astype(jnp.bfloat16)
    keys = prepare_head(key_pre, gains[5], cosine, sine).astype(jnp.bfloat16)
    values = value_pre.astype(jnp.bfloat16)
    marks = (segment_ids + 1).astype(jnp.bfloat16)
    key_parts, value_parts, mark_parts = ([], [], [])
    step = 1
    moved = from_behind((keys, values, marks), "dp", step)
    key_parts.append(moved[0])
    value_parts.append(moved[1])
    mark_parts.append(moved[2])
    all_keys = jnp.concatenate(key_parts + [keys], axis=0)
    all_values = jnp.concatenate(value_parts + [values], axis=0)
    all_marks = jnp.concatenate(mark_parts + [marks], axis=0)

    def block_parts(start):
        first_key = start + reach * length - WINDOW
        visible = inside & (marks[:, None] == all_marks[None, :])
        product = (
            jnp.einsum("qd,kd->qk", queries, all_keys, preferred_element_type=jnp.float32)
            * score_scale
        )
        return (first_key, queries, all_keys, all_values, jnp.where(visible, product, NEG))

    mixed_parts, total_parts = ([], [])
    start = 0
    first_key, query_block, key_block, value_block, scores = block_parts(start)
    highest = jnp.max(scores, axis=-1, keepdims=True)
    expo = jnp.exp(scores - highest)
    denominator = jnp.sum(expo, axis=-1, keepdims=True)
    probs = (expo / denominator).astype(jnp.bfloat16)
    mixed_parts.append(jnp.dot(probs, value_block, preferred_element_type=jnp.float32))
    total_parts.append(highest + jnp.log(denominator))
    attended = mixed_parts[0].astype(jnp.bfloat16)
    log_totals = total_parts[0]
    attn_out = scatter_ordered(
        jnp.einsum("le,de->ld", attended, output_turned, preferred_element_type=jnp.float32).astype(
            jnp.bfloat16
        )
    )
    middle = residual + normalize(attn_out, gains[1])
    ff_local = normalize(middle, gains[2]).astype(jnp.bfloat16)
    ff_in = jnp.concatenate(gather_relative(ff_local), axis=0)
    gate = jnp.dot(ff_in, gate_up_full[0], preferred_element_type=jnp.float32)
    up_part = jnp.dot(ff_in, gate_up_full[1], preferred_element_type=jnp.float32)
    hidden = gated_units(gate, up_part).astype(jnp.bfloat16)
    ff_out = scatter_relative(
        split_rows(
            jnp.dot(hidden, down_full, preferred_element_type=jnp.float32).astype(jnp.bfloat16)
        )
    )
    result = (middle + normalize(ff_out, gains[3])).astype(jnp.bfloat16)
    top_grad = out_grad.astype(jnp.float32)
    ff_out_grad, ff_post_grad = norm_back(ff_out, gains[3], top_grad)
    ff_grad_all = jnp.concatenate(gather_relative(ff_out_grad.astype(jnp.bfloat16)), axis=0)
    hidden_grad = jnp.einsum(
        "ld,fd->lf", ff_grad_all, down_full, preferred_element_type=jnp.float32
    )
    down_grad_turned = jnp.einsum(
        "ld,lf->df", ff_grad_all, hidden, preferred_element_type=jnp.float32
    )
    unused, unit_pull = jax.vjp(gated_units, gate, up_part)
    gate_grad, up_grad = unit_pull(hidden_grad)
    gate_low = gate_grad.astype(jnp.bfloat16)
    up_low = up_grad.astype(jnp.bfloat16)
    gate_turned = jnp.einsum("ld,lf->df", ff_in, gate_low, preferred_element_type=jnp.float32)
    up_turned = jnp.einsum("ld,lf->df", ff_in, up_low, preferred_element_type=jnp.float32)
    ff_in_partial = (
        jnp.einsum("lf,df->ld", gate_low, gate_up_full[0], preferred_element_type=jnp.float32)
        + jnp.einsum("lf,df->ld", up_low, gate_up_full[1], preferred_element_type=jnp.float32)
    ).astype(jnp.bfloat16)
    ff_in_partial, down_low, gate_turned_low, up_turned_low = lax.optimization_barrier(
        (
            ff_in_partial,
            down_grad_turned.astype(jnp.bfloat16),
            gate_turned.astype(jnp.bfloat16),
            up_turned.astype(jnp.bfloat16),
        )
    )
    feed_forward_owned = tuple(
        (
            lax.psum_scatter(item, "dp", scatter_dimension=0, tiled=True)
            for item in (down_low, gate_turned_low, up_turned_low)
        )
    )
    ff_in_grad = scatter_relative(split_rows(ff_in_partial))
    middle_part, ff_pre_grad = norm_back(middle, gains[2], ff_in_grad)
    middle_grad = top_grad + middle_part
    attn_out_grad, attn_post_grad = norm_back(attn_out, gains[1], middle_grad)
    attn_grad_all = gather_ordered(attn_out_grad.astype(jnp.bfloat16))
    attended_grad = jnp.einsum(
        "ld,de->le", attn_grad_all, output_turned, preferred_element_type=jnp.float32
    ).astype(jnp.bfloat16)
    output_grad_turned = jnp.einsum(
        "ld,le->de", attn_grad_all, attended, preferred_element_type=jnp.float32
    )
    key_grad_all = jnp.zeros(((reach + 1) * length, head_size), jnp.float32)
    value_grad_all = jnp.zeros(((reach + 1) * length, head_size), jnp.float32)
    start = 0
    first_key, query_block, key_block, value_block, scores = block_parts(start)
    probs = jnp.exp(scores - log_totals)
    probs_low = probs.astype(jnp.bfloat16)
    value_grad_all = value_grad_all.at[first_key : first_key + span].add(
        jnp.einsum("qk,qd->kd", probs_low, attended_grad, preferred_element_type=jnp.float32)
    )
    prob_grad = jnp.einsum(
        "qd,kd->qk", attended_grad, value_block, preferred_element_type=jnp.float32
    )
    inner = jnp.sum(probs * prob_grad, axis=-1, keepdims=True)
    score_grad = (probs * (prob_grad - inner)).astype(jnp.bfloat16)
    query_parts = jnp.dot(score_grad, key_block, preferred_element_type=jnp.float32) * score_scale
    key_grad_all = key_grad_all.at[first_key : first_key + span].add(
        jnp.einsum("qk,qd->kd", score_grad, query_block, preferred_element_type=jnp.float32)
        * score_scale
    )
    own_keys = key_grad_all[reach * length :]
    own_values = value_grad_all[reach * length :]
    step = 1
    slot = reach - step
    returned = (
        from_behind(
            key_grad_all[slot * length : (slot + 1) * length].astype(jnp.bfloat16), "dp", -step
        ).astype(jnp.float32),
        from_behind(
            value_grad_all[slot * length : (slot + 1) * length].astype(jnp.bfloat16), "dp", -step
        ).astype(jnp.float32),
    )
    own_keys = own_keys + returned[0]
    own_values = own_values + returned[1]
    unused, query_pull = jax.vjp(
        partial(prepare_head, cosine=cosine, sine=sine), query_pre, gains[4]
    )
    query_pre_grad, query_gain_grad = query_pull(query_parts)
    unused, key_pull = jax.vjp(partial(prepare_head, cosine=cosine, sine=sine), key_pre, gains[5])
    key_pre_grad, key_gain_grad = key_pull(own_keys)
    joint_grad_rows = jnp.concatenate([query_pre_grad, key_pre_grad, own_values], axis=1).astype(
        jnp.bfloat16
    )
    joint_grad = jnp.einsum(
        "ld,lc->dc", attn_in, joint_grad_rows, preferred_element_type=jnp.float32
    )
    attn_in_grad = scatter_ordered(
        jnp.einsum(
            "lc,dc->ld", joint_grad_rows, joint_weight, preferred_element_type=jnp.float32
        ).astype(jnp.bfloat16)
    )
    tokens_part, attn_pre_grad = norm_back(residual, gains[0], attn_in_grad)
    tokens_grad = middle_grad + tokens_part
    small_grads = [
        jnp.pad(item.reshape(-1, gain_rows), ((0, 0), (0, rows - gain_rows))).reshape(-1)
        for item in (query_gain_grad, key_gain_grad)
    ]
    gain_grads = jnp.stack(
        [attn_pre_grad, attn_post_grad, ff_pre_grad, ff_post_grad] + small_grads, axis=1
    )
    gain_grads = jnp.pad(gain_grads, ((0, 0), (0, 128 - gain_grads.shape[1])))
    packed_grad = jnp.concatenate(
        [
            joint_grad[:, :head_size].astype(jnp.bfloat16),
            output_grad_turned.astype(jnp.bfloat16),
            joint_grad[:, head_size:].astype(jnp.bfloat16),
            gain_grads.astype(jnp.bfloat16),
        ],
        axis=1,
    )
    packed_grad, feed_forward_owned = lax.optimization_barrier((packed_grad, feed_forward_owned))
    down_owned = jnp.transpose(feed_forward_owned[0]).astype(jnp.float32)
    gate_up_owned = jnp.stack(feed_forward_owned[1:], axis=0).astype(jnp.float32)
    packed_owned = lax.psum_scatter(packed_grad, "dp", scatter_dimension=0, tiled=True)
    query_owned = packed_owned[:, :head_size].astype(jnp.float32)
    output_owned = jnp.transpose(packed_owned[:, head_size : 2 * head_size]).astype(jnp.float32)
    summed = sum_over_mp(packed_owned[:, 2 * head_size :])
    keyval_owned = summed[:, : 2 * head_size]
    gain_owned = jnp.transpose(summed[:, 2 * head_size :])
    return (
        result,
        tokens_grad,
        query_owned,
        keyval_owned,
        output_owned,
        gate_up_owned,
        down_owned,
        gain_owned[0],
        gain_owned[1],
        gain_owned[2],
        gain_owned[3],
        gain_owned[4, :gain_rows],
        gain_owned[5, :gain_rows],
    )


def solution(mesh):
    placed = (
        P(("dp", "mp"), None),
        P("dp"),
        P("dp"),
        P("dp", "mp"),
        P("dp", None),
        P("mp", "dp"),
        P(None, "dp", "mp"),
        P("mp", "dp"),
        P("dp"),
        P("dp"),
        P("dp"),
        P("dp"),
        P("dp"),
        P("dp"),
        P(("dp", "mp"), None),
    )
    return jax.shard_map(
        local,
        mesh=mesh,
        in_specs=placed,
        out_specs=(
            P(("dp", "mp"), None),
            P(("dp", "mp"), None),
            P("dp", "mp"),
            P("dp", None),
            P("mp", "dp"),
            P(None, "dp", "mp"),
            P("mp", "dp"),
            P("dp"),
            P("dp"),
            P("dp"),
            P("dp"),
            P("dp"),
            P("dp"),
        ),
        check_vma=False,
    )
```

profile of v0, /device:TPU:0, one launch (start us, length us, event | category | flops | bytes accessed | tf_op | source)
XLA Modules:
  0.0 732.3 jit_solution(13621012869615528322)
XLA Ops:
  14.2 56.9 %all-gather.4.cloned.1.call-done = bf16[1152,1152]{1,0:T(8,128)(2,1)} async-done(((bf16[144,1152]{1,0:T(8,128)(2,1)}), bf16[1152,1152]{1,0:T(8,128)(2,1)}) %all-gather.4.cloned.1.call-update) | async-done | bytes 2654224 | tf_op jit(solution)/shard_map/all_gather | solution.py:131
  76.5 3.9 collective-permute-done.1
  80.4 9.1 %collective-permute-done.2 = bf16[128,1152]{1,0:T(8,128)(2,1)S(1)} collective-permute-done((bf16[128,1152]{1,0:T(8,128)(2,1)S(1)}, bf16[128,1152]{1,0:T(8,128)(2,1)S(1)}, u32[]{:S(2)}, u32[]{:S(2)}) %collective-permute-start.2) | collective-permute-done | bytes 294944 | tf_op jit(solution)/shard_map/ppermute | solution.py:20
  97.4 4.3 collective-permute-start
  103.1 10.1 %collective-permute-start.5 = (bf16[512,256]{1,0:T(8,128)(2,1)S(1)}, bf16[512,256]{1,0:T(8,128)(2,1)S(1)}, u32[]{:S(2)}, u32[]{:S(2)}) collective-permute-start(bf16[512,256]{1,0:T(8,128)(2,1)S(1)} %slice.321), channel_id=1, source_target_pairs={{0,4},{4,8},{8,12},{12,16},{16,20},{20,24},{24,28},{1,5},{5,9},{9,... | collective-permute-start | bytes 786440 | tf_op jit(solution)/shard_map/ppermute | solution.py:15
  120.8 5.7 collective-permute-done.8
  126.5 7.6 %collective-permute-done.7 = bf16[128,1152]{1,0:T(8,128)(2,1)S(1)} collective-permute-done((bf16[128,1152]{1,0:T(8,128)(2,1)S(1)}, bf16[128,1152]{1,0:T(8,128)(2,1)S(1)}, u32[]{:S(2)}, u32[]{:S(2)}) %collective-permute-start.7) | collective-permute-done | bytes 294944 | tf_op jit(solution)/shard_map/ppermute | solution.py:20
  138.2 6.0 collective-permute-done.11
  149.7 54.7 %all-gather.6.cloned.1.call-done = bf16[2,1152,1728]{2,1,0:T(8,128)(2,1)} async-done(((bf16[2,144,1728]{2,1,0:T(8,128)(2,1)}), bf16[2,1152,1728]{2,1,0:T(8,128)(2,1)}) %all-gather.6.cloned.1.call-update) | async-done | bytes 7962640 | tf_op jit(solution)/shard_map/all_gather | solution.py:132
  204.4 5.2 fusion.2
  211.4 6.8 multiply_convert_fusion.1
  218.2 59.2 %all-gather.8.cloned.1.call-done = bf16[1728,1152]{0,1:T(8,128)(2,1)} async-done(((bf16[1728,144]{0,1:T(8,128)(2,1)}), bf16[1728,1152]{0,1:T(8,128)(2,1)}) %all-gather.8.cloned.1.call-update) | async-done | bytes 3981328 | tf_op jit(solution)/shard_map/all_gather | solution.py:133
  277.4 5.3 convolution_convert_fusion.5
  284.6 4.7 collective-permute-done.14
  289.2 9.2 %collective-permute-done.13 = bf16[128,1152]{1,0:T(8,128)(2,1)S(1)} collective-permute-done((bf16[128,1152]{1,0:T(8,128)(2,1)S(1)}, bf16[128,1152]{1,0:T(8,128)(2,1)S(1)}, u32[]{:S(2)}, u32[]{:S(2)}) %collective-permute-start.13) | collective-permute-done | bytes 294944 | tf_op jit(solution)/shard_map/ppermute | solution.py:20
  302.6 6.7 collective-permute-done.17
  314.3 4.3 convolution_convert_fusion.2
  318.6 8.4 %multiply_convert_fusion = (bf16[512,1728]{0,1:T(8,128)(2,1)S(1)}, bf16[512,1728]{0,1:T(8,128)(2,1)S(1)}) fusion(f32[512,1728]{0,1:T(8,128)S(1)} %copy-done.77, f32[512,1728]{0,1:T(8,128)} %get-tuple-element.185, bf16[1728,1152]{0,1:T(8,128)(2,1)S(1)} %copy-done.67, bf16[128,1152]{1,0:T(8,128)(2,1)S(1)} %collective-permute-done.17, ...), kind=kOutput, calls=%fused_computation.20 | convolution fusion | flops 2064384000 | bytes 15777792 | tf_op jit(solution)/shard_map/ld,fd->lf/dot_general | solution.py:213
  329.7 5.4 convolution_convert_fusion.1
  335.1 5.3 convolution_convert_fusion
  344.1 6.5 copy.60
  350.7 6.5 copy.62
  362.7 6.5 copy.64
  369.2 7.4 %collective-permute-done.19 = bf16[128,1152]{1,0:T(8,128)(2,1)} collective-permute-done((bf16[128,1152]{1,0:T(8,128)(2,1)}, bf16[128,1152]{1,0:T(8,128)(2,1)}, u32[]{:S(2)}, u32[]{:S(2)}) %collective-permute-start.19) | collective-permute-done | bytes 294944 | tf_op jit(solution)/shard_map/ppermute | solution.py:20
  383.5 4.9 collective-permute-done.21
  388.4 6.6 collective-permute-done.22
  403.9 13.7 %collective-permute-done.24 = bf16[512,256]{1,0:T(8,128)(2,1)S(1)} collective-permute-done((bf16[512,256]{1,0:T(8,128)(2,1)S(1)}, bf16[512,256]{1,0:T(8,128)(2,1)S(1)}, u32[]{:S(2)}, u32[]{:S(2)}) %collective-permute-start.24) | collective-permute-done | bytes 262176 | tf_op jit(solution)/shard_map/ppermute | solution.py:15
  442.1 4.6 reduce-scatter.13.cloned.1.call-done
  449.0 89.0 %reduce-scatter.15.cloned.1.call-done = bf16[144,1728]{1,0:T(8,128)(2,1)} async-done(((bf16[1152,1728]{1,0:T(8,128)(2,1)}), bf16[144,1728]{1,0:T(8,128)(2,1)}) %reduce-scatter.15.cloned.1.call-update) | async-done | bytes 497680
  540.2 88.7 %reduce-scatter.17.cloned.1.call-done = bf16[144,1728]{1,0:T(8,128)(2,1)} async-done(((bf16[1152,1728]{1,0:T(8,128)(2,1)}), bf16[144,1728]{1,0:T(8,128)(2,1)}) %reduce-scatter.17.cloned.1.call-update) | async-done | bytes 497680
  642.2 62.7 %reduce-scatter.19.cloned.1.call-done = bf16[144,1152]{1,0:T(8,128)(2,1)} async-done(((bf16[1152,1152]{1,0:T(8,128)(2,1)}), bf16[144,1152]{1,0:T(8,128)(2,1)}) %reduce-scatter.19.cloned.1.call-update) | async-done | bytes 331792
  713.1 9.9 %collective-permute-done.30 = bf16[144,640]{0,1:T(8,128)(2,1)S(1)} collective-permute-done((bf16[144,640]{0,1:T(8,128)(2,1)S(1)}, bf16[144,640]{0,1:T(8,128)(2,1)S(1)}, u32[]{:S(2)}, u32[]{:S(2)}) %collective-permute-start.30) | collective-permute-done | bytes 184352 | tf_op jit(solution)/shard_map/ppermute | solution.py:20
  (352 shorter events, 131.0 us)
Async XLA Ops:
  7.2 63.9 %all-gather.4.cloned.1.call-start = ((), (), s32[]{:S(2)}) async-start(), calls=%async_computation.4 | async-start | bytes 2985984 | tf_op jit(solution)/shard_map/all_gather | solution.py:131
  13.2 191.2 %all-gather.6.cloned.1.call-start = ((), (), s32[]{:S(2)}) async-start(), calls=%async_computation.5 | async-start | bytes 9289728 | tf_op jit(solution)/shard_map/all_gather | solution.py:132
  13.9 263.5 %all-gather.8.cloned.1.call-start = ((), (), s32[]{:S(2)}) async-start(), calls=%async_computation.6 | async-start | bytes 4644864 | tf_op jit(solution)/shard_map/all_gather | solution.py:133
  74.2 372.5 %reduce-scatter.13.cloned.1.call-start = ((), (), s32[]{:S(2)}) async-start(), calls=%async_computation.7 | async-start | bytes 4644864
  74.5 15.0 %collective-permute-start.2 = (bf16[128,1152]{1,0:T(8,128)(2,1)S(1)}, bf16[128,1152]{1,0:T(8,128)(2,1)S(1)}, u32[]{:S(2)}, u32[]{:S(2)}) collective-permute-start(bf16[128,1152]{1,0:T(8,128)(2,1)S(1)} %get-tuple-element.141), channel_id=1, source_target_pairs={{0,2},{1,3},{2,0},{3,1},{4,6},{5,7},{6,4},{7,5},{8,10},{9,11},{10,... | collective-permute-start | bytes 884744 | tf_op jit(solution)/shard_map/ppermute | solution.py:20
  76.0 13.8 %collective-permute-start.3 = (bf16[128,1152]{1,0:T(8,128)(2,1)S(1)}, bf16[128,1152]{1,0:T(8,128)(2,1)S(1)}, u32[]{:S(2)}, u32[]{:S(2)}) collective-permute-start(bf16[128,1152]{1,0:T(8,128)(2,1)S(1)} %get-tuple-element.141), channel_id=1, source_target_pairs={{0,1},{1,2},{2,3},{3,0},{4,5},{5,6},{6,7},{7,4},{8,9},{9,10},{10,1... | collective-permute-start | bytes 884744 | tf_op jit(solution)/shard_map/ppermute | solution.py:20
  94.9 18.2 %collective-permute-start.4 = (bf16[512,256]{1,0:T(8,128)(2,1)S(1)}, bf16[512,256]{1,0:T(8,128)(2,1)S(1)}, u32[]{:S(2)}, u32[]{:S(2)}) collective-permute-start(bf16[512,256]{1,0:T(8,128)(2,1)S(1)} %pad_maximum_fusion.9), channel_id=1, source_target_pairs={{0,4},{4,8},{8,12},{12,16},{16,20},{20,24},{24,28},{1,5},{5,9},{9,... | collective-permute-start | bytes 786440 | tf_op jit(solution)/shard_map/ppermute | solution.py:15
  103.1 13.9 %collective-permute-start.5 = (bf16[512,256]{1,0:T(8,128)(2,1)S(1)}, bf16[512,256]{1,0:T(8,128)(2,1)S(1)}, u32[]{:S(2)}, u32[]{:S(2)}) collective-permute-start(bf16[512,256]{1,0:T(8,128)(2,1)S(1)} %slice.321), channel_id=1, source_target_pairs={{0,4},{4,8},{8,12},{12,16},{16,20},{20,24},{24,28},{1,5},{5,9},{9,... | collective-permute-start | bytes 786440 | tf_op jit(solution)/shard_map/ppermute | solution.py:15
  119.6 14.6 %collective-permute-start.7 = (bf16[128,1152]{1,0:T(8,128)(2,1)S(1)}, bf16[128,1152]{1,0:T(8,128)(2,1)S(1)}, u32[]{:S(2)}, u32[]{:S(2)}) collective-permute-start(bf16[128,1152]{1,0:T(8,128)(2,1)S(1)} %get-tuple-element.159), channel_id=1, source_target_pairs={{0,2},{1,3},{2,0},{3,1},{4,6},{5,7},{6,4},{7,5},{8,10},{9,11},{10,... | collective-permute-start | bytes 884744 | tf_op jit(solution)/shard_map/ppermute | solution.py:20
  120.6 14.1 %collective-permute-start.6 = (bf16[128,1152]{1,0:T(8,128)(2,1)S(1)}, bf16[128,1152]{1,0:T(8,128)(2,1)S(1)}, u32[]{:S(2)}, u32[]{:S(2)}) collective-permute-start(bf16[128,1152]{1,0:T(8,128)(2,1)S(1)} %get-tuple-element.157), channel_id=1, source_target_pairs={{0,1},{1,2},{2,3},{3,0},{4,5},{5,6},{6,7},{7,4},{8,9},{9,10},{10,1... | collective-permute-start | bytes 884744 | tf_op jit(solution)/shard_map/ppermute | solution.py:20
  135.5 9.9 %collective-permute-start.10 = (bf16[128,1152]{1,0:T(8,128)(2,1)S(1)}, bf16[128,1152]{1,0:T(8,128)(2,1)S(1)}, u32[]{:S(2)}, u32[]{:S(2)}) collective-permute-start(bf16[128,1152]{1,0:T(8,128)(2,1)S(1)} %multiply_convert_fusion.3), channel_id=1, source_target_pairs={{0,2},{1,3},{2,0},{3,1},{4,6},{5,7},{6,4},{7,5},{8,10},{9,11},{10,... | collective-permute-start | bytes 884744 | tf_op jit(solution)/shard_map/ppermute | solution.py:20
  136.7 13.1 %collective-permute-start.9 = (bf16[128,1152]{1,0:T(8,128)(2,1)S(1)}, bf16[128,1152]{1,0:T(8,128)(2,1)}, u32[]{:S(2)}, u32[]{:S(2)}) collective-permute-start(bf16[128,1152]{1,0:T(8,128)(2,1)S(1)} %multiply_convert_fusion.3), channel_id=1, source_target_pairs={{0,3},{1,0},{2,1},{3,2},{4,7},{5,4},{6,5},{7,6},{8,11},{9,8},{10,9... | collective-permute-start | bytes 884744 | tf_op jit(solution)/shard_map/ppermute | solution.py:20
  282.9 15.5 %collective-permute-start.13 = (bf16[128,1152]{1,0:T(8,128)(2,1)S(1)}, bf16[128,1152]{1,0:T(8,128)(2,1)S(1)}, u32[]{:S(2)}, u32[]{:S(2)}) collective-permute-start(bf16[128,1152]{1,0:T(8,128)(2,1)S(1)} %get-tuple-element.156), channel_id=1, source_target_pairs={{0,2},{1,3},{2,0},{3,1},{4,6},{5,7},{6,4},{7,5},{8,10},{9,11},{10,... | collective-permute-start | bytes 884744 | tf_op jit(solution)/shard_map/ppermute | solution.py:20
  284.4 14.1 %collective-permute-start.12 = (bf16[128,1152]{1,0:T(8,128)(2,1)S(1)}, bf16[128,1152]{1,0:T(8,128)(2,1)S(1)}, u32[]{:S(2)}, u32[]{:S(2)}) collective-permute-start(bf16[128,1152]{1,0:T(8,128)(2,1)S(1)} %get-tuple-element.154), channel_id=1, source_target_pairs={{0,1},{1,2},{2,3},{3,0},{4,5},{5,6},{6,7},{7,4},{8,9},{9,10},{10,1... | collective-permute-start | bytes 884744 | tf_op jit(solution)/shard_map/ppermute | solution.py:20
  300.5 8.8 %collective-permute-start.17 = (bf16[128,1152]{1,0:T(8,128)(2,1)S(1)}, bf16[128,1152]{1,0:T(8,128)(2,1)S(1)}, u32[]{:S(2)}, u32[]{:S(2)}) collective-permute-start(bf16[128,1152]{1,0:T(8,128)(2,1)S(1)} %get-tuple-element.160), channel_id=1, source_target_pairs={{0,1},{1,2},{2,3},{3,0},{4,5},{5,6},{6,7},{7,4},{8,9},{9,10},{10,1... | collective-permute-start | bytes 884744 | tf_op jit(solution)/shard_map/ppermute | solution.py:20
  300.6 9.9 %collective-permute-start.16 = (bf16[128,1152]{1,0:T(8,128)(2,1)S(1)}, bf16[128,1152]{1,0:T(8,128)(2,1)S(1)}, u32[]{:S(2)}, u32[]{:S(2)}) collective-permute-start(bf16[128,1152]{1,0:T(8,128)(2,1)S(1)} %get-tuple-element.160), channel_id=1, source_target_pairs={{0,2},{1,3},{2,0},{3,1},{4,6},{5,7},{6,4},{7,5},{8,10},{9,11},{10,... | collective-permute-start | bytes 884744 | tf_op jit(solution)/shard_map/ppermute | solution.py:20
  301.1 13.1 %collective-permute-start.15 = (bf16[128,1152]{1,0:T(8,128)(2,1)S(1)}, bf16[128,1152]{1,0:T(8,128)(2,1)S(1)}, u32[]{:S(2)}, u32[]{:S(2)}) collective-permute-start(bf16[128,1152]{1,0:T(8,128)(2,1)S(1)} %get-tuple-element.160), channel_id=1, source_target_pairs={{0,3},{1,0},{2,1},{3,2},{4,7},{5,4},{6,5},{7,6},{8,11},{9,8},{10,9... | collective-permute-start | bytes 884744 | tf_op jit(solution)/shard_map/ppermute | solution.py:20
  350.6 187.4 %reduce-scatter.15.cloned.1.call-start = ((), (), s32[]{:S(2)}) async-start(), calls=%async_computation.8 | async-start | bytes 4644864
  357.2 271.7 %reduce-scatter.17.cloned.1.call-start = ((), (), s32[]{:S(2)}) async-start(), calls=%async_computation.9 | async-start | bytes 4644864
  359.4 9.9 %collective-permute-start.20 = (bf16[128,1152]{1,0:T(8,128)(2,1)}, bf16[128,1152]{1,0:T(8,128)(2,1)}, u32[]{:S(2)}, u32[]{:S(2)}) collective-permute-start(bf16[128,1152]{1,0:T(8,128)(2,1)} %get-tuple-element.152), channel_id=1, source_target_pairs={{0,3},{1,0},{2,1},{3,2},{4,7},{5,4},{6,5},{7,6},{8,11},{9,8},{10,9... | collective-permute-start | bytes 884744 | tf_op jit(solution)/shard_map/ppermute | solution.py:20
  361.2 15.4 %collective-permute-start.19 = (bf16[128,1152]{1,0:T(8,128)(2,1)}, bf16[128,1152]{1,0:T(8,128)(2,1)}, u32[]{:S(2)}, u32[]{:S(2)}) collective-permute-start(bf16[128,1152]{1,0:T(8,128)(2,1)} %get-tuple-element.153), channel_id=1, source_target_pairs={{0,2},{1,3},{2,0},{3,1},{4,6},{5,7},{6,4},{7,5},{8,10},{9,11},{10,... | collective-permute-start | bytes 884744 | tf_op jit(solution)/shard_map/ppermute | solution.py:20
  362.7 14.0 %collective-permute-start.18 = (bf16[128,1152]{1,0:T(8,128)(2,1)}, bf16[128,1152]{1,0:T(8,128)(2,1)}, u32[]{:S(2)}, u32[]{:S(2)}) collective-permute-start(bf16[128,1152]{1,0:T(8,128)(2,1)} %get-tuple-element.151), channel_id=1, source_target_pairs={{0,1},{1,2},{2,3},{3,0},{4,5},{5,6},{6,7},{7,4},{8,9},{9,10},{10,1... | collective-permute-start | bytes 884744 | tf_op jit(solution)/shard_map/ppermute | solution.py:20
  369.2 335.7 %reduce-scatter.19.cloned.1.call-start = ((), (), s32[]{:S(2)}) async-start(), calls=%async_computation.10 | async-start | bytes 2985984
  381.2 13.8 %collective-permute-start.22 = (bf16[128,1152]{1,0:T(8,128)(2,1)S(1)}, bf16[128,1152]{1,0:T(8,128)(2,1)S(1)}, u32[]{:S(2)}, u32[]{:S(2)}) collective-permute-start(bf16[128,1152]{1,0:T(8,128)(2,1)S(1)} %get-tuple-element.132), channel_id=1, source_target_pairs={{0,2},{1,3},{2,0},{3,1},{4,6},{5,7},{6,4},{7,5},{8,10},{9,11},{10,... | collective-permute-start | bytes 884744 | tf_op jit(solution)/shard_map/ppermute | solution.py:20
  381.9 14.1 %collective-permute-start.23 = (bf16[128,1152]{1,0:T(8,128)(2,1)S(1)}, bf16[128,1152]{1,0:T(8,128)(2,1)S(1)}, u32[]{:S(2)}, u32[]{:S(2)}) collective-permute-start(bf16[128,1152]{1,0:T(8,128)(2,1)S(1)} %get-tuple-element.132), channel_id=1, source_target_pairs={{0,1},{1,2},{2,3},{3,0},{4,5},{5,6},{6,7},{7,4},{8,9},{9,10},{10,1... | collective-permute-start | bytes 884744 | tf_op jit(solution)/shard_map/ppermute | solution.py:20
  397.2 22.6 %collective-permute-start.25 = (bf16[512,256]{1,0:T(8,128)(2,1)S(1)}, bf16[512,256]{1,0:T(8,128)(2,1)S(1)}, u32[]{:S(2)}, u32[]{:S(2)}) collective-permute-start(bf16[512,256]{1,0:T(8,128)(2,1)S(1)} %slice.319), channel_id=1, source_target_pairs={{4,0},{8,4},{12,8},{16,12},{20,16},{24,20},{28,24},{5,1},{9,5},{13... | collective-permute-start | bytes 786440 | tf_op jit(solution)/shard_map/ppermute | solution.py:15
  400.6 16.9 %collective-permute-start.24 = (bf16[512,256]{1,0:T(8,128)(2,1)S(1)}, bf16[512,256]{1,0:T(8,128)(2,1)S(1)}, u32[]{:S(2)}, u32[]{:S(2)}) collective-permute-start(bf16[512,256]{1,0:T(8,128)(2,1)S(1)} %slice.320), channel_id=1, source_target_pairs={{4,0},{8,4},{12,8},{16,12},{20,16},{24,20},{28,24},{5,1},{9,5},{13... | collective-permute-start | bytes 786440 | tf_op jit(solution)/shard_map/ppermute | solution.py:15
  421.6 11.8 %collective-permute-start.28 = (bf16[128,1152]{1,0:T(8,128)(2,1)S(1)}, bf16[128,1152]{1,0:T(8,128)(2,1)S(1)}, u32[]{:S(2)}, u32[]{:S(2)}) collective-permute-start(bf16[128,1152]{1,0:T(8,128)(2,1)S(1)} %get-tuple-element.149), channel_id=1, source_target_pairs={{0,3},{1,0},{2,1},{3,2},{4,7},{5,4},{6,5},{7,6},{8,11},{9,8},{10,9... | collective-permute-start | bytes 884744 | tf_op jit(solution)/shard_map/ppermute | solution.py:20
  421.7 13.8 %collective-permute-start.27 = (bf16[128,1152]{1,0:T(8,128)(2,1)S(1)}, bf16[128,1152]{1,0:T(8,128)(2,1)S(1)}, u32[]{:S(2)}, u32[]{:S(2)}) collective-permute-start(bf16[128,1152]{1,0:T(8,128)(2,1)S(1)} %get-tuple-element.150), channel_id=1, source_target_pairs={{0,2},{1,3},{2,0},{3,1},{4,6},{5,7},{6,4},{7,5},{8,10},{9,11},{10,... | collective-permute-start | bytes 884744 | tf_op jit(solution)/shard_map/ppermute | solution.py:20
  422.3 14.2 %collective-permute-start.26 = (bf16[128,1152]{1,0:T(8,128)(2,1)S(1)}, bf16[128,1152]{1,0:T(8,128)(2,1)}, u32[]{:S(2)}, u32[]{:S(2)}) collective-permute-start(bf16[128,1152]{1,0:T(8,128)(2,1)S(1)} %get-tuple-element.148), channel_id=1, source_target_pairs={{0,1},{1,2},{2,3},{3,0},{4,5},{5,6},{6,7},{7,4},{8,9},{9,10},{10,1... | collective-permute-start | bytes 884744 | tf_op jit(solution)/shard_map/ppermute | solution.py:20
  706.1 16.9 %collective-permute-start.30 = (bf16[144,640]{0,1:T(8,128)(2,1)S(1)}, bf16[144,640]{0,1:T(8,128)(2,1)S(1)}, u32[]{:S(2)}, u32[]{:S(2)}) collective-permute-start(bf16[144,640]{0,1:T(8,128)(2,1)S(1)} %copy.69), channel_id=1, source_target_pairs={{0,2},{1,3},{2,0},{3,1},{4,6},{5,7},{6,4},{7,5},{8,10},{9,11},{10,... | collective-permute-start | bytes 552968 | tf_op jit(solution)/shard_map/ppermute | solution.py:20
  707.6 15.5 %collective-permute-start.29 = (bf16[144,640]{0,1:T(8,128)(2,1)S(1)}, bf16[144,640]{0,1:T(8,128)(2,1)S(1)}, u32[]{:S(2)}, u32[]{:S(2)}) collective-permute-start(bf16[144,640]{0,1:T(8,128)(2,1)S(1)} %copy.69), channel_id=1, source_target_pairs={{0,1},{1,2},{2,3},{3,0},{4,5},{5,6},{6,7},{7,4},{8,9},{9,10},{10,1... | collective-permute-start | bytes 552968 | tf_op jit(solution)/shard_map/ppermute | solution.py:20
  (89 other events, 816.2 us)
Sparse Core Ops, SparseCore 0:
  13.3 57.7 all-gather.3
  73.3 131.1 all-gather.5
  206.6 70.7 all-gather.7
  350.7 95.9 reduce-scatter.12
  450.5 87.4 reduce-scatter.14
  541.4 87.4 reduce-scatter.16
  634.6 70.2 reduce-scatter.18
where the time goes:
time: 740 us; the launch traced here: 732 us
  waiting for transfers between devices  533 us (72%)
  local copies, waits for them, and re-layouts  65.2 us (9%)
  matrix products  59.8 us (8%)
  starting transfers between devices  36.2 us (5%)
  other arithmetic  22.5 us (3%)
  between operations  15.8 us (2%)
    unnamed x11, waiting for transfers between devices  246 us
    ppermute x27, waiting for transfers between devices, shifted(): lax.ppermute(value, axis, [(i, (i + shift) % count) for i in range(count)])  99.2 us
    all_gather x1, waiting for transfers between devices, local(): down_full = lax.all_gather(down_weight, 'dp', axis=1, tiled=True)  59.2 us
    all_gather x1, waiting for transfers between devices, local(): packed_full = lax.all_gather(packed, 'dp', axis=0, tiled=True)  56.9 us
    all_gather x1, waiting for transfers between devices, local(): gate_up_full = lax.all_gather(gate_up_weight, 'dp', axis=1, tiled=True)  54.7 us
    unnamed x175, local copies, waits for them, and re-layouts  34.6 us
    ppermute x5, starting transfers between devices, from_behind(): lax.ppermute(value, axis, [(source, source + steps) for source in range(l...  19.4 us
    ppermute x5, waiting for transfers between devices, from_behind(): lax.ppermute(value, axis, [(source, source + steps) for source in range(l...  17.3 us
  transfers between devices with their start and end apart: 39, of which 34 were waited for; matrix products, arithmetic and copies ran while one was open for 11% of the time, Pallas kernels for 0%

commit v1 on v0

--- a/solution.py
+++ b/solution.py
@@ -3,10 +3,18 @@
 import jax.numpy as jnp
 from jax import lax
 from jax.sharding import PartitionSpec as P
+from jax.lax import axis_index, axis_size, ppermute
 
 WINDOW = 512
 EPS = 1e-06
 NEG = -1e30
+
+
+def scan_the_region(tile_in, ndim_at):
+    current_block = list(tile_in.shape[1:])
+    current_block[ndim_at] *= tile_in.shape[0]
+    p_next = jnp.moveaxis(tile_in, 0, ndim_at).reshape(current_block)
+    return p_next
 
 
 def from_behind(value, axis, steps):
@@ -129,7 +137,22 @@
     gain_columns = jnp.pad(gain_columns, ((0, 0), (0, 128 - gain_columns.shape[1])))
     packed = jnp.concatenate([q_weight, kv_weight, jnp.transpose(o_weight), gain_columns], axis=1)
     packed_full = lax.all_gather(packed, "dp", axis=0, tiled=True)
-    gate_up_full = lax.all_gather(gate_up_weight, "dp", axis=1, tiled=True)
+    q_n = axis_size("dp")
+    vals = tuple(((s, (s + 1) % q_n) for s in range(q_n)))
+    ledger = tuple(((d, w) for w, d in vals))
+    k_now, then = ([], [])
+    for dev_j in [*range(q_n - 1)]:
+        if dev_j % 2 == 0:
+            k_now.append(
+                ppermute(k_now[-1] if k_now else gate_up_weight, axis_name="dp", perm=vals)
+            )
+        else:
+            then.append(ppermute(then[-1] if then else gate_up_weight, axis_name="dp", perm=ledger))
+    ready = jnp.stack([*k_now[::-1], gate_up_weight, *then], axis=0)
+    fresh = axis_index("dp")
+    block_last = fresh - len(k_now)
+    ready = ready[(jnp.arange(q_n) - block_last) % q_n]
+    gate_up_full = scan_the_region(ready, 1)
     down_full = lax.all_gather(down_weight, "dp", axis=1, tiled=True)
     joint_weight = packed_full[:, : 3 * head_size]
     output_turned = packed_full[:, 3 * head_size : 4 * head_size]

time: 740 us -> 759 us (1.026)
  local copies, waits for them, and re-layouts: 65.2 us -> 91.8 us
  waiting for transfers between devices: 533 us -> 519 us
    ppermute x0 -> x7, waiting for transfers between devices: none -> 137 us  [the longest x4 137 us: local(): ppermute(k_now[-1] if k_now else gate_up_weight, axis_name='dp', perm=vals)]
    all_gather x1, waiting for transfers between devices: 59.2 us -> 0.01 us  [local(): down_full = lax.all_gather(down_weight, 'dp', axis=1, tiled=True)]
    all_gather x1, waiting for transfers between devices: 56.9 us -> 0.01 us  [local(): packed_full = lax.all_gather(packed, 'dp', axis=0, tiled=True)]
    all_gather x1 -> x0, waiting for transfers between devices: 54.7 us -> none  [local(): gate_up_full = lax.all_gather(gate_up_weight, 'dp', axis=1, tiled=True)]
    ppermute x5, waiting for transfers between devices: 17.3 us -> 50.9 us  [from_behind(): lax.ppermute(value, axis, [(source, source + steps) for source in range(l...]
    ppermute x0 -> x7, starting transfers between devices: none -> 16.2 us  [the longest x3 8.14 us: local(): ppermute(then[-1] if then else gate_up_weight, axis_name='dp', perm=ledger)]
    ppermute x27, waiting for transfers between devices: 99.2 us -> 85.2 us  [shifted(): lax.ppermute(value, axis, [(i, (i + shift) % count) for i in range(count)])]
    unnamed x175 -> x182, local copies, waits for them, and re-layouts: 34.6 us -> 47.3 us
  transfers between devices with their start and end apart: 39 -> 45, of which waited for: 34 -> 34; matrix products, arithmetic and copies ran while one was open for 11% -> 15% of each run, Pallas kernels for 0% -> 0%
where the time goes in v1:
time: 759 us; the launch traced here: 750 us
  waiting for transfers between devices  519 us (68%)
  local copies, waits for them, and re-layouts  91.8 us (12%)
  matrix products  53.2 us (7%)
  starting transfers between devices  43.5 us (6%)
  other arithmetic  27 us (4%)
  between operations  15.7 us (2%)
    unnamed x10, waiting for transfers between devices  245 us
    ppermute x4, waiting for transfers between devices, local(): ppermute(k_now[-1] if k_now else gate_up_weight, axis_name='dp', perm=vals)  137 us
    ppermute x27, waiting for transfers between devices, shifted(): lax.ppermute(value, axis, [(i, (i + shift) % count) for i in range(count)])  85.2 us
    ppermute x5, waiting for transfers between devices, from_behind(): lax.ppermute(value, axis, [(source, source + steps) for source in range(l...  50.9 us
    unnamed x182, local copies, waits for them, and re-layouts  47.3 us
    ppermute x27, starting transfers between devices, shifted(): lax.ppermute(value, axis, [(i, (i + shift) % count) for i in range(count)])  16.6 us
  transfers between devices with their start and end apart: 45, of which 34 were waited for; matrix products, arithmetic and copies ran while one was open for 15% of the time, Pallas kernels for 0%

profile of v1, /device:TPU:0, one launch (start us, length us, event | category | flops | bytes accessed | tf_op | source)
XLA Modules:
  0.0 749.9 jit_solution(10566087925165221907)
XLA Ops:
  16.2 36.8 %collective-permute-done.12 = bf16[2,144,1728]{2,1,0:T(8,128)(2,1)S(1)} collective-permute-done((bf16[2,144,1728]{2,1,0:T(8,128)(2,1)}, bf16[2,144,1728]{2,1,0:T(8,128)(2,1)S(1)}, u32[]{:S(2)}, u32[]{:S(2)}) %collective-permute-start.12) | collective-permute-done | bytes 995360 | tf_op jit(solution)/shard_map/ppermute | solution.py:147
  53.0 4.7 collective-permute-start.16
  57.7 53.4 %collective-permute-done.13 = bf16[2,144,1728]{2,1,0:T(8,128)(2,1)S(1)} collective-permute-done((bf16[2,144,1728]{2,1,0:T(8,128)(2,1)S(1)}, bf16[2,144,1728]{2,1,0:T(8,128)(2,1)S(1)}, u32[]{:S(2)}, u32[]{:S(2)}) %collective-permute-start.13) | collective-permute-done | bytes 995360 | tf_op jit(solution)/shard_map/ppermute | solution.py:147
  115.9 40.9 %collective-permute-done.14 = bf16[2,144,1728]{2,1,0:T(8,128)(2,1)} collective-permute-done((bf16[2,144,1728]{2,1,0:T(8,128)(2,1)S(1)}, bf16[2,144,1728]{2,1,0:T(8,128)(2,1)}, u32[]{:S(2)}, u32[]{:S(2)}) %collective-permute-start.14) | collective-permute-done | bytes 995360 | tf_op jit(solution)/shard_map/ppermute | solution.py:147
  164.5 21.9 %collective-permute-done = bf16[512]{0:T(512)(128)(2,1)S(1)} collective-permute-done((bf16[512]{0:T(512)(128)(2,1)S(1)}, bf16[512]{0:T(512)(128)(2,1)S(1)}, u32[]{:S(2)}, u32[]{:S(2)}) %collective-permute-start) | collective-permute-done | bytes 1056 | tf_op jit(solution)/shard_map/ppermute | solution.py:23
  187.6 6.3 collective-permute-done.15
  206.7 5.4 collective-permute-done.1
  212.1 6.2 collective-permute-done.2
  233.0 8.0 %collective-permute-done.4 = bf16[512,256]{1,0:T(8,128)(2,1)S(1)} collective-permute-done((bf16[512,256]{1,0:T(8,128)(2,1)S(1)}, bf16[512,256]{1,0:T(8,128)(2,1)S(1)}, u32[]{:S(2)}, u32[]{:S(2)}) %collective-permute-start.4) | collective-permute-done | bytes 262176 | tf_op jit(solution)/shard_map/ppermute | solution.py:23
  242.5 6.5 collective-permute-done.5
  256.1 8.1 %gather_fusion = bf16[8,2,144,1728]{3,2,1,0:T(8,128)(2,1)} fusion(bf16[8,2,144,1728]{3,2,1,0:T(8,128)(2,1)} %bitcast_dynamic-update-slice_fusion, s32[1024]{0:T(1024)S(1)} %pad_clamp_fusion), kind=kCustom, calls=%fused_computation | custom fusion | bytes 15925280 | tf_op jit(solution)/shard_map/gather | solution.py:154
  289.7 6.4 multiply_convert_fusion.1
  296.1 5.4 convolution_convert_fusion.5
  304.9 6.0 collective-permute-done.21
  310.9 7.7 %collective-permute-done.20 = bf16[128,1152]{1,0:T(8,128)(2,1)S(1)} collective-permute-done((bf16[128,1152]{1,0:T(8,128)(2,1)S(1)}, bf16[128,1152]{1,0:T(8,128)(2,1)S(1)}, u32[]{:S(2)}, u32[]{:S(2)}) %collective-permute-start.20) | collective-permute-done | bytes 294944 | tf_op jit(solution)/shard_map/ppermute | solution.py:28
  322.8 6.6 collective-permute-done.24
  334.5 6.6 multiply_convert_fusion
  347.5 4.4 convolution_convert_fusion.2
  351.9 4.5 convolution_convert_fusion.1
  356.3 4.3 convolution_convert_fusion
  360.7 6.5 copy.60
  367.2 6.4 copy.62
  379.5 6.5 copy.64
  386.1 7.4 collective-permute-done.26
  400.3 4.8 collective-permute-done.28
  405.1 7.0 collective-permute-done.29
  420.8 14.5 %collective-permute-done.31 = bf16[512,256]{1,0:T(8,128)(2,1)S(1)} collective-permute-done((bf16[512,256]{1,0:T(8,128)(2,1)S(1)}, bf16[512,256]{1,0:T(8,128)(2,1)S(1)}, u32[]{:S(2)}, u32[]{:S(2)}) %collective-permute-start.31) | collective-permute-done | bytes 262176 | tf_op jit(solution)/shard_map/ppermute | solution.py:23
  459.8 4.3 reduce-scatter.13.cloned.1.call-done
  466.4 89.0 %reduce-scatter.15.cloned.1.call-done = bf16[144,1728]{1,0:T(8,128)(2,1)} async-done(((bf16[1152,1728]{1,0:T(8,128)(2,1)}), bf16[144,1728]{1,0:T(8,128)(2,1)}) %reduce-scatter.15.cloned.1.call-update) | async-done | bytes 497680
  557.6 88.6 %reduce-scatter.17.cloned.1.call-done = bf16[144,1728]{1,0:T(8,128)(2,1)} async-done(((bf16[1152,1728]{1,0:T(8,128)(2,1)}), bf16[144,1728]{1,0:T(8,128)(2,1)}) %reduce-scatter.17.cloned.1.call-update) | async-done | bytes 497680
  659.4 63.3 %reduce-scatter.19.cloned.1.call-done = bf16[144,1152]{1,0:T(8,128)(2,1)} async-done(((bf16[1152,1152]{1,0:T(8,128)(2,1)}), bf16[144,1152]{1,0:T(8,128)(2,1)}) %reduce-scatter.19.cloned.1.call-update) | async-done | bytes 331792
  731.4 9.0 %collective-permute-done.37 = bf16[144,640]{0,1:T(8,128)(2,1)S(1)} collective-permute-done((bf16[144,640]{0,1:T(8,128)(2,1)S(1)}, bf16[144,640]{0,1:T(8,128)(2,1)S(1)}, u32[]{:S(2)}, u32[]{:S(2)}) %collective-permute-start.37) | collective-permute-done | bytes 184352 | tf_op jit(solution)/shard_map/ppermute | solution.py:28
  (374 shorter events, 177.0 us)
Async XLA Ops:
  7.2 194.4 %all-gather.3.cloned.1.call-start = ((), (), s32[]{:S(2)}) async-start(), calls=%async_computation.4 | async-start | bytes 2985984 | tf_op jit(solution)/shard_map/all_gather | solution.py:139
  13.1 283.0 %all-gather.5.cloned.1.call-start = ((), (), s32[]{:S(2)}) async-start(), calls=%async_computation.5 | async-start | bytes 4644864 | tf_op jit(solution)/shard_map/all_gather | solution.py:156
  13.2 39.8 %collective-permute-start.12 = (bf16[2,144,1728]{2,1,0:T(8,128)(2,1)}, bf16[2,144,1728]{2,1,0:T(8,128)(2,1)S(1)}, u32[]{:S(2)}, u32[]{:S(2)}) collective-permute-start(bf16[2,144,1728]{2,1,0:T(8,128)(2,1)} %param.29), channel_id=1, source_target_pairs={{0,4},{4,8},{8,12},{12,16},{16,20},{20,24},{24,28},{28,0},{1,5},{5... | collective-permute-start | bytes 2985992 | tf_op jit(solution)/shard_map/ppermute | solution.py:147
  53.0 58.1 %collective-permute-start.13 = (bf16[2,144,1728]{2,1,0:T(8,128)(2,1)S(1)}, bf16[2,144,1728]{2,1,0:T(8,128)(2,1)S(1)}, u32[]{:S(2)}, u32[]{:S(2)}) collective-permute-start(bf16[2,144,1728]{2,1,0:T(8,128)(2,1)S(1)} %collective-permute-done.12), channel_id=1, source_target_pairs={{0,4},{4,8},{8,12},{12,16},{16,20},{20,24},{24,28},{28,0},{1,5},{5... | collective-permute-start | bytes 2985992 | tf_op jit(solution)/shard_map/ppermute | solution.py:147
  53.0 60.6 %collective-permute-start.16 = (bf16[2,144,1728]{2,1,0:T(8,128)(2,1)}, bf16[2,144,1728]{2,1,0:T(8,128)(2,1)S(1)}, u32[]{:S(2)}, u32[]{:S(2)}) collective-permute-start(bf16[2,144,1728]{2,1,0:T(8,128)(2,1)} %param.29), channel_id=1, source_target_pairs={{4,0},{8,4},{12,8},{16,12},{20,16},{24,20},{28,24},{0,28},{5,1},{9... | collective-permute-start | bytes 2985992 | tf_op jit(solution)/shard_map/ppermute | solution.py:150
  111.1 45.6 %collective-permute-start.14 = (bf16[2,144,1728]{2,1,0:T(8,128)(2,1)S(1)}, bf16[2,144,1728]{2,1,0:T(8,128)(2,1)}, u32[]{:S(2)}, u32[]{:S(2)}) collective-permute-start(bf16[2,144,1728]{2,1,0:T(8,128)(2,1)S(1)} %collective-permute-done.13), channel_id=1, source_target_pairs={{0,4},{4,8},{8,12},{12,16},{16,20},{20,24},{24,28},{28,0},{1,5},{5... | collective-permute-start | bytes 2985992 | tf_op jit(solution)/shard_map/ppermute | solution.py:147
  113.6 72.8 %collective-permute-start.17 = (bf16[2,144,1728]{2,1,0:T(8,128)(2,1)S(1)}, bf16[2,144,1728]{2,1,0:T(8,128)(2,1)}, u32[]{:S(2)}, u32[]{:S(2)}) collective-permute-start(bf16[2,144,1728]{2,1,0:T(8,128)(2,1)S(1)} %collective-permute-done.16), channel_id=1, source_target_pairs={{4,0},{8,4},{12,8},{16,12},{20,16},{24,20},{28,24},{0,28},{5,1},{9... | collective-permute-start | bytes 2985992 | tf_op jit(solution)/shard_map/ppermute | solution.py:150
  156.8 37.1 %collective-permute-start.15 = (bf16[2,144,1728]{2,1,0:T(8,128)(2,1)}, bf16[2,144,1728]{2,1,0:T(8,128)(2,1)}, u32[]{:S(2)}, u32[]{:S(2)}) collective-permute-start(bf16[2,144,1728]{2,1,0:T(8,128)(2,1)} %collective-permute-done.14), channel_id=1, source_target_pairs={{0,4},{4,8},{8,12},{12,16},{16,20},{20,24},{24,28},{28,0},{1,5},{5... | collective-permute-start | bytes 2985992 | tf_op jit(solution)/shard_map/ppermute | solution.py:147
  160.1 26.4 %collective-permute-start = (bf16[512]{0:T(512)(128)(2,1)S(1)}, bf16[512]{0:T(512)(128)(2,1)S(1)}, u32[]{:S(2)}, u32[]{:S(2)}) collective-permute-start(bf16[512]{0:T(512)(128)(2,1)S(1)} %add_convert_fusion.1), channel_id=1, source_target_pairs={{0,4},{4,8},{8,12},{12,16},{16,20},{20,24},{24,28},{1,5},{5,9},{9,... | collective-permute-start | bytes 3080 | tf_op jit(solution)/shard_map/ppermute | solution.py:23
  162.0 302.1 %reduce-scatter.13.cloned.1.call-start = ((), (), s32[]{:S(2)}) async-start(), calls=%async_computation.6 | async-start | bytes 4644864
  186.5 67.4 %collective-permute-start.18 = (bf16[2,144,1728]{2,1,0:T(8,128)(2,1)}, bf16[2,144,1728]{2,1,0:T(8,128)(2,1)}, u32[]{:S(2)}, u32[]{:S(2)}) collective-permute-start(bf16[2,144,1728]{2,1,0:T(8,128)(2,1)} %collective-permute-done.17), channel_id=1, source_target_pairs={{4,0},{8,4},{12,8},{16,12},{20,16},{24,20},{28,24},{0,28},{5,1},{9... | collective-permute-start | bytes 2985992 | tf_op jit(solution)/shard_map/ppermute | solution.py:150
  204.7 13.7 %collective-permute-start.2 = (bf16[128,1152]{1,0:T(8,128)(2,1)S(1)}, bf16[128,1152]{1,0:T(8,128)(2,1)S(1)}, u32[]{:S(2)}, u32[]{:S(2)}) collective-permute-start(bf16[128,1152]{1,0:T(8,128)(2,1)S(1)} %get-tuple-element.141), channel_id=1, source_target_pairs={{0,2},{1,3},{2,0},{3,1},{4,6},{5,7},{6,4},{7,5},{8,10},{9,11},{10,... | collective-permute-start | bytes 884744 | tf_op jit(solution)/shard_map/ppermute | solution.py:28
  225.1 15.9 %collective-permute-start.4 = (bf16[512,256]{1,0:T(8,128)(2,1)S(1)}, bf16[512,256]{1,0:T(8,128)(2,1)S(1)}, u32[]{:S(2)}, u32[]{:S(2)}) collective-permute-start(bf16[512,256]{1,0:T(8,128)(2,1)S(1)} %pad_maximum_fusion.9), channel_id=1, source_target_pairs={{0,4},{4,8},{8,12},{12,16},{16,20},{20,24},{24,28},{1,5},{5,9},{9,... | collective-permute-start | bytes 786440 | tf_op jit(solution)/shard_map/ppermute | solution.py:23
  228.7 20.2 %collective-permute-start.5 = (bf16[512,256]{1,0:T(8,128)(2,1)S(1)}, bf16[512,256]{1,0:T(8,128)(2,1)S(1)}, u32[]{:S(2)}, u32[]{:S(2)}) collective-permute-start(bf16[512,256]{1,0:T(8,128)(2,1)S(1)} %slice.315), channel_id=1, source_target_pairs={{0,4},{4,8},{8,12},{12,16},{16,20},{20,24},{24,28},{1,5},{5,9},{9,... | collective-permute-start | bytes 786440 | tf_op jit(solution)/shard_map/ppermute | solution.py:23
  252.5 15.4 %collective-permute-start.7 = (bf16[128,1152]{1,0:T(8,128)(2,1)S(1)}, bf16[128,1152]{1,0:T(8,128)(2,1)}, u32[]{:S(2)}, u32[]{:S(2)}) collective-permute-start(bf16[128,1152]{1,0:T(8,128)(2,1)S(1)} %get-tuple-element.161), channel_id=1, source_target_pairs={{0,2},{1,3},{2,0},{3,1},{4,6},{5,7},{6,4},{7,5},{8,10},{9,11},{10,... | collective-permute-start | bytes 884744 | tf_op jit(solution)/shard_map/ppermute | solution.py:28
  253.8 14.3 %collective-permute-start.6 = (bf16[128,1152]{1,0:T(8,128)(2,1)S(1)}, bf16[128,1152]{1,0:T(8,128)(2,1)}, u32[]{:S(2)}, u32[]{:S(2)}) collective-permute-start(bf16[128,1152]{1,0:T(8,128)(2,1)S(1)} %get-tuple-element.159), channel_id=1, source_target_pairs={{0,1},{1,2},{2,3},{3,0},{4,5},{5,6},{6,7},{7,4},{8,9},{9,10},{10,1... | collective-permute-start | bytes 884744 | tf_op jit(solution)/shard_map/ppermute | solution.py:28
  303.6 15.0 %collective-permute-start.20 = (bf16[128,1152]{1,0:T(8,128)(2,1)S(1)}, bf16[128,1152]{1,0:T(8,128)(2,1)S(1)}, u32[]{:S(2)}, u32[]{:S(2)}) collective-permute-start(bf16[128,1152]{1,0:T(8,128)(2,1)S(1)} %get-tuple-element.158), channel_id=1, source_target_pairs={{0,2},{1,3},{2,0},{3,1},{4,6},{5,7},{6,4},{7,5},{8,10},{9,11},{10,... | collective-permute-start | bytes 884744 | tf_op jit(solution)/shard_map/ppermute | solution.py:28
  304.9 13.7 %collective-permute-start.19 = (bf16[128,1152]{1,0:T(8,128)(2,1)S(1)}, bf16[128,1152]{1,0:T(8,128)(2,1)S(1)}, u32[]{:S(2)}, u32[]{:S(2)}) collective-permute-start(bf16[128,1152]{1,0:T(8,128)(2,1)S(1)} %get-tuple-element.156), channel_id=1, source_target_pairs={{0,1},{1,2},{2,3},{3,0},{4,5},{5,6},{6,7},{7,4},{8,9},{9,10},{10,1... | collective-permute-start | bytes 884744 | tf_op jit(solution)/shard_map/ppermute | solution.py:28
  321.4 13.1 %collective-permute-start.22 = (bf16[128,1152]{1,0:T(8,128)(2,1)S(1)}, bf16[128,1152]{1,0:T(8,128)(2,1)S(1)}, u32[]{:S(2)}, u32[]{:S(2)}) collective-permute-start(bf16[128,1152]{1,0:T(8,128)(2,1)S(1)} %get-tuple-element.162), channel_id=1, source_target_pairs={{0,3},{1,0},{2,1},{3,2},{4,7},{5,4},{6,5},{7,6},{8,11},{9,8},{10,9... | collective-permute-start | bytes 884744 | tf_op jit(solution)/shard_map/ppermute | solution.py:28
  367.2 188.2 %reduce-scatter.15.cloned.1.call-start = ((), (), s32[]{:S(2)}) async-start(), calls=%async_computation.7 | async-start | bytes 4644864
  373.7 272.5 %reduce-scatter.17.cloned.1.call-start = ((), (), s32[]{:S(2)}) async-start(), calls=%async_computation.8 | async-start | bytes 4644864
  378.1 15.3 %collective-permute-start.26 = (bf16[128,1152]{1,0:T(8,128)(2,1)}, bf16[128,1152]{1,0:T(8,128)(2,1)}, u32[]{:S(2)}, u32[]{:S(2)}) collective-permute-start(bf16[128,1152]{1,0:T(8,128)(2,1)} %get-tuple-element.155), channel_id=1, source_target_pairs={{0,2},{1,3},{2,0},{3,1},{4,6},{5,7},{6,4},{7,5},{8,10},{9,11},{10,... | collective-permute-start | bytes 884744 | tf_op jit(solution)/shard_map/ppermute | solution.py:28
  379.5 14.0 %collective-permute-start.25 = (bf16[128,1152]{1,0:T(8,128)(2,1)}, bf16[128,1152]{1,0:T(8,128)(2,1)}, u32[]{:S(2)}, u32[]{:S(2)}) collective-permute-start(bf16[128,1152]{1,0:T(8,128)(2,1)} %get-tuple-element.153), channel_id=1, source_target_pairs={{0,1},{1,2},{2,3},{3,0},{4,5},{5,6},{6,7},{7,4},{8,9},{9,10},{10,1... | collective-permute-start | bytes 884744 | tf_op jit(solution)/shard_map/ppermute | solution.py:28
  386.0 336.7 %reduce-scatter.19.cloned.1.call-start = ((), (), s32[]{:S(2)}) async-start(), calls=%async_computation.9 | async-start | bytes 2985984
  398.0 14.1 %collective-permute-start.29 = (bf16[128,1152]{1,0:T(8,128)(2,1)S(1)}, bf16[128,1152]{1,0:T(8,128)(2,1)S(1)}, u32[]{:S(2)}, u32[]{:S(2)}) collective-permute-start(bf16[128,1152]{1,0:T(8,128)(2,1)S(1)} %get-tuple-element.132), channel_id=1, source_target_pairs={{0,2},{1,3},{2,0},{3,1},{4,6},{5,7},{6,4},{7,5},{8,10},{9,11},{10,... | collective-permute-start | bytes 884744 | tf_op jit(solution)/shard_map/ppermute | solution.py:28
  398.9 14.1 %collective-permute-start.30 = (bf16[128,1152]{1,0:T(8,128)(2,1)S(1)}, bf16[128,1152]{1,0:T(8,128)(2,1)S(1)}, u32[]{:S(2)}, u32[]{:S(2)}) collective-permute-start(bf16[128,1152]{1,0:T(8,128)(2,1)S(1)} %get-tuple-element.132), channel_id=1, source_target_pairs={{0,1},{1,2},{2,3},{3,0},{4,5},{5,6},{6,7},{7,4},{8,9},{9,10},{10,1... | collective-permute-start | bytes 884744 | tf_op jit(solution)/shard_map/ppermute | solution.py:28
  414.2 23.4 %collective-permute-start.32 = (bf16[512,256]{1,0:T(8,128)(2,1)S(1)}, bf16[512,256]{1,0:T(8,128)(2,1)S(1)}, u32[]{:S(2)}, u32[]{:S(2)}) collective-permute-start(bf16[512,256]{1,0:T(8,128)(2,1)S(1)} %slice.313), channel_id=1, source_target_pairs={{4,0},{8,4},{12,8},{16,12},{20,16},{24,20},{28,24},{5,1},{9,5},{13... | collective-permute-start | bytes 786440 | tf_op jit(solution)/shard_map/ppermute | solution.py:23
  417.6 17.7 %collective-permute-start.31 = (bf16[512,256]{1,0:T(8,128)(2,1)S(1)}, bf16[512,256]{1,0:T(8,128)(2,1)S(1)}, u32[]{:S(2)}, u32[]{:S(2)}) collective-permute-start(bf16[512,256]{1,0:T(8,128)(2,1)S(1)} %slice.314), channel_id=1, source_target_pairs={{4,0},{8,4},{12,8},{16,12},{20,16},{24,20},{28,24},{5,1},{9,5},{13... | collective-permute-start | bytes 786440 | tf_op jit(solution)/shard_map/ppermute | solution.py:23
  439.4 13.6 %collective-permute-start.34 = (bf16[128,1152]{1,0:T(8,128)(2,1)S(1)}, bf16[128,1152]{1,0:T(8,128)(2,1)S(1)}, u32[]{:S(2)}, u32[]{:S(2)}) collective-permute-start(bf16[128,1152]{1,0:T(8,128)(2,1)S(1)} %get-tuple-element.152), channel_id=1, source_target_pairs={{0,2},{1,3},{2,0},{3,1},{4,6},{5,7},{6,4},{7,5},{8,10},{9,11},{10,... | collective-permute-start | bytes 884744 | tf_op jit(solution)/shard_map/ppermute | solution.py:28
  440.0 14.2 %collective-permute-start.33 = (bf16[128,1152]{1,0:T(8,128)(2,1)S(1)}, bf16[128,1152]{1,0:T(8,128)(2,1)}, u32[]{:S(2)}, u32[]{:S(2)}) collective-permute-start(bf16[128,1152]{1,0:T(8,128)(2,1)S(1)} %get-tuple-element.150), channel_id=1, source_target_pairs={{0,1},{1,2},{2,3},{3,0},{4,5},{5,6},{6,7},{7,4},{8,9},{9,10},{10,1... | collective-permute-start | bytes 884744 | tf_op jit(solution)/shard_map/ppermute | solution.py:28
  723.9 16.4 %collective-permute-start.37 = (bf16[144,640]{0,1:T(8,128)(2,1)S(1)}, bf16[144,640]{0,1:T(8,128)(2,1)S(1)}, u32[]{:S(2)}, u32[]{:S(2)}) collective-permute-start(bf16[144,640]{0,1:T(8,128)(2,1)S(1)} %copy.69), channel_id=1, source_target_pairs={{0,2},{1,3},{2,0},{3,1},{4,6},{5,7},{6,4},{7,5},{8,10},{9,11},{10,... | collective-permute-start | bytes 552968 | tf_op jit(solution)/shard_map/ppermute | solution.py:28
  725.2 15.5 %collective-permute-start.36 = (bf16[144,640]{0,1:T(8,128)(2,1)S(1)}, bf16[144,640]{0,1:T(8,128)(2,1)S(1)}, u32[]{:S(2)}, u32[]{:S(2)}) collective-permute-start(bf16[144,640]{0,1:T(8,128)(2,1)S(1)} %copy.69), channel_id=1, source_target_pairs={{0,1},{1,2},{2,3},{3,0},{4,5},{5,6},{6,7},{7,4},{8,9},{9,10},{10,1... | collective-permute-start | bytes 552968 | tf_op jit(solution)/shard_map/ppermute | solution.py:28
  (95 other events, 916.1 us)
Sparse Core Ops, SparseCore 0:
  13.3 101.8 all-gather.2
  162.1 95.8 all-gather.4
  367.3 96.7 reduce-scatter.12
  467.9 87.3 reduce-scatter.14
  558.8 87.3 reduce-scatter.16
  651.9 70.8 reduce-scatter.18
